TPU v7x, 128 devices: a whole 4x4x4 slice. The times are simulated.
128 devices in a mesh: rows: 32 (over z, x_hi, y), feat: 4 (over x_lo, core).
Axes of the slice: x: 4 (x_hi: 2, x_lo: 2; x = x_hi * 2 + x_lo), y: 4, z: 4, core: 2. Of those that a mesh axis runs over, the one named last changes fastest.
Arguments:
- slab: float32 [16384, 2048], P('rows', 'feat'), may hold values from -42 to 42
- cov_old: float32 [2048, 2048], P('rows', 'feat'), may hold values from -4.5 to 4.5, as said below
Outputs:
- whitened: float32 [16384, 2048], P('rows', 'feat')
- factor: float32 [2048, 2048], P('rows', 'feat')
Inputs may be any that keep to these rules, and one draw needn't show every extreme that they name: `cov_old`: symmetric.
All inputs are finite; a program needn't handle non-finite values.
Results may differ from a plain program's by a relative error of at most 0.000098.
Values sent between devices are 32-bit elements; how exact they have to be, the bound alone decides.
A program may use at most 192 MiB of HBM per device.

v0:
```python
import jax
import jax.numpy as jnp
from jax import lax
from jax.sharding import PartitionSpec as P


def broadcast(shard, axis, root):
    mine = lax.axis_index(axis) == root
    return lax.psum(jnp.where(mine, shard, jnp.zeros_like(shard)), axis)


def matmul(left, right):
    return jnp.dot(left, right, precision=lax.Precision.HIGHEST, preferred_element_type=jnp.float32)


def invert_diag(diag_factor):
    identity = jnp.eye(diag_factor.shape[0], dtype=jnp.float32)
    return lax.linalg.triangular_solve(diag_factor, identity, left_side=True, lower=True)


def invert_lower(factor_full, width, n_feat):
    diag_inverses = []
    for block in range(n_feat):
        low = block * width
        diag_inverses.append(invert_diag(factor_full[low : low + width, low : low + width]))
    dim = width * n_feat
    inverse = jnp.zeros((dim, dim), jnp.float32)
    for col in range(n_feat):
        cl = col * width
        known = diag_inverses[col]
        inverse = inverse.at[cl : cl + width, cl : cl + width].set(known)
        for row in range(col + 1, n_feat):
            rl = row * width
            partial_sum = matmul(
                factor_full[rl : rl + width, cl:rl], inverse[cl:rl, cl : cl + width]
            )
            inverse = inverse.at[rl : rl + width, cl : cl + width].set(
                -matmul(diag_inverses[row], partial_sum)
            )
    return inverse


def per_device(slab, cov_old):
    n_rows = lax.axis_size("rows")
    n_feat = lax.axis_size("feat")
    row_index = lax.axis_index("rows")
    feat_index = lax.axis_index("feat")
    rows_dev, width = slab.shape
    dim = width * n_feat
    total = rows_dev * n_rows
    cov_rows = cov_old.shape[0]
    column_sums = lax.psum(jnp.sum(slab, axis=0), "rows")
    centered = slab - (column_sums / total)[None, :]
    full_rows = lax.all_gather(centered, "feat", axis=1, tiled=True)
    contract = (((0,), (0,)), ((), ()))
    own_rows = lax.psum_scatter(
        lax.dot_general(
            full_rows,
            centered,
            contract,
            precision=lax.Precision.HIGHEST,
            preferred_element_type=jnp.float32,
        )
        / total,
        "rows",
        scatter_dimension=0,
        tiled=True,
    )
    column = lax.all_gather(cov_old + own_rows, "rows", axis=0, tiled=True)
    factor_full = jnp.zeros((dim, dim), jnp.float32)
    identity = jnp.eye(width, dtype=jnp.float32)
    for step in range(n_feat):
        lower_part = column[step * width :]
        is_root = feat_index == step
        diag_block = jnp.where(is_root, lower_part[:width], identity)
        below = jnp.where(is_root, lower_part, 0.0)
        diag_factor = jnp.tril(lax.linalg.cholesky(diag_block))
        diag_inverse = invert_diag(diag_factor)
        panel_local = lax.dot_general(
            below,
            diag_inverse,
            (((1,), (1,)), ((), ())),
            precision=lax.Precision.HIGHEST,
            preferred_element_type=jnp.float32,
        )
        panel_all = broadcast(panel_local, "feat", step)
        factor_full = factor_full.at[step * width :, step * width : (step + 1) * width].set(
            panel_all
        )
        if step + 1 < n_feat:
            span = panel_all.shape[0]
            start = jnp.clip((feat_index - step) * width, 0, span - width)
            partner = lax.dynamic_slice_in_dim(panel_all, start, width, 0)
            update = lax.dot_general(
                panel_all,
                partner,
                (((1,), (1,)), ((), ())),
                precision=lax.Precision.HIGHEST,
                preferred_element_type=jnp.float32,
            )
            update = jnp.where(feat_index > step, update, 0.0)
            column = column.at[step * width :].add(-update)
    inverse = invert_lower(factor_full, width, n_feat)
    quarter = rows_dev // n_feat
    my_rows = lax.dynamic_slice_in_dim(full_rows, feat_index * quarter, quarter, 0)
    solved = lax.dot_general(
        my_rows,
        inverse,
        (((1,), (1,)), ((), ())),
        precision=lax.Precision.HIGHEST,
        preferred_element_type=jnp.float32,
    )
    whitened = lax.all_to_all(solved, "feat", split_axis=1, concat_axis=0, tiled=True)
    factor_rows = lax.dynamic_slice_in_dim(factor_full, row_index * cov_rows, cov_rows, 0)
    factor_out = lax.dynamic_slice_in_dim(factor_rows, feat_index * width, width, 1)
    return (whitened, factor_out)


def solution(mesh):
    placed = (P("rows", "feat"), P("rows", "feat"))
    return jax.shard_map(
        per_device,
        mesh=mesh,
        in_specs=placed,
        out_specs=(P("rows", "feat"), P("rows", "feat")),
        check_vma=False,
    )
```

profile of v0, /device:TPU:7, one launch (start us, length us, event | category | flops | bytes accessed | tf_op | source)
XLA Modules:
  0.0 1698.0 jit_solution(12982457571958026488)
XLA Ops:
  8.5 73.1 %psum.35 = f32[512]{0:T(512)S(1)} all-reduce(f32[512]{0:T(512)S(1)} %reduce_sum.9), channel_id=1, replica_groups=mesh['rows'=32,'feat'=4] {'rows'}, use_global_device_ids=true, to_apply=%region_1.0 | all-reduce | flops 512 | bytes 4096 | tf_op jit(solution)/shard_map/psum | solution.py:52
  84.0 65.0 %all-gather.3.cloned.1.call-done = f32[512,2048]{1,0:T(8,128)} async-done(((f32[512,512]{1,0:T(8,128)}), f32[512,2048]{1,0:T(8,128)}) %all-gather.3.cloned.1.call-update) | async-done | bytes 4194320 | tf_op jit(solution)/shard_map/all_gather | solution.py:54
  149.0 10.1 convolution_multiply_fusion
  159.1 159.8 %reduce-scatter.4.cloned.1.call-done = f32[64,512]{1,0:T(8,128)} async-done(((f32[2048,512]{1,0:T(8,128)}), f32[64,512]{1,0:T(8,128)}) %reduce-scatter.4.cloned.1.call-update) | async-done | bytes 131088 | tf_op jit(solution)/shard_map/reduce_scatter | solution.py:56
  320.7 109.1 %all-gather.5.cloned.1.call-done = f32[2048,512]{1,0:T(8,128)} async-done(((f32[64,512]{1,0:T(8,128)}), f32[2048,512]{1,0:T(8,128)}) %all-gather.5.cloned.1.call-update) | async-done | bytes 4194320 | tf_op jit(solution)/shard_map/all_gather | solution.py:69
  439.6 11.7 custom-call.55
  451.4 9.8 custom-call.56
  464.1 11.7 custom-call.57
  475.9 10.2 custom-call.58
  487.9 11.7 custom-call.59
  511.3 11.9 custom-call.61
  536.5 39.3 %custom-call.62 = f32[4,128,128]{1,2,0:T(8,128)S(1)} custom-call(f32[4,128,128]{2,1,0:T(8,128)S(1)} %get-tuple-element.266), custom_call_target="InvertDiagBlocksLowerTriangular" | custom-call | tf_op jit(solution)/shard_map/triangular_solve/custom-call.3 | solution.py:18
  589.3 92.1 %all-reduce.8.cloned.1.call-done = f32[2048,512]{0,1:T(8,128)} async-done(((f32[2048,512]{0,1:T(8,128)}), f32[2048,512]{0,1:T(8,128)}) %all-reduce.8.cloned.1.call-update) | async-done | bytes 4194320 | tf_op jit(solution)/shard_map/psum | solution.py:9
  681.4 10.4 negate_add_fusion
  696.8 11.7 custom-call.63
  708.6 9.8 custom-call.64
  721.3 11.7 custom-call.65
  733.1 10.0 custom-call.66
  744.8 11.7 custom-call.67
  768.3 12.1 custom-call.69
  793.8 39.3 %custom-call.70 = f32[4,128,128]{1,2,0:T(8,128)S(1)} custom-call(f32[4,128,128]{2,1,0:T(8,128)S(1)} %get-tuple-element.267), custom_call_target="InvertDiagBlocksLowerTriangular" | custom-call | tf_op jit(solution)/shard_map/triangular_solve/custom-call.3 | solution.py:18
  845.1 75.5 %all-reduce.10.cloned.1.call-done = f32[1536,512]{0,1:T(8,128)} async-done(((f32[1536,512]{0,1:T(8,128)}), f32[1536,512]{0,1:T(8,128)}) %all-reduce.10.cloned.1.call-update) | async-done | bytes 3145744 | tf_op jit(solution)/shard_map/psum | solution.py:9
  934.1 11.7 custom-call.71
  945.9 9.8 custom-call.72
  958.6 11.7 custom-call.73
  970.5 10.2 custom-call.74
  982.5 11.7 custom-call.75
  1005.8 11.9 custom-call.77
  1032.1 39.3 %custom-call.78 = f32[4,128,128]{1,2,0:T(8,128)S(1)} custom-call(f32[4,128,128]{2,1,0:T(8,128)S(1)} %get-tuple-element.268), custom_call_target="InvertDiagBlocksLowerTriangular" | custom-call | tf_op jit(solution)/shard_map/triangular_solve/custom-call.3 | solution.py:18
  1085.3 54.5 %all-reduce.12.cloned.1.call-done = f32[1024,512]{0,1:T(8,128)} async-done(((f32[1024,512]{0,1:T(8,128)}), f32[1024,512]{0,1:T(8,128)}) %all-reduce.12.cloned.1.call-update) | async-done | bytes 2097168 | tf_op jit(solution)/shard_map/psum | solution.py:9
  1150.3 11.7 custom-call.79
  1173.0 12.1 custom-call.81
  1196.0 11.7 custom-call.83
  1207.9 10.0 custom-call.84
  1218.6 11.7 custom-call.85
  1236.9 12.3 while.37
  1250.0 40.3 %custom-call.86 = f32[4,128,128]{1,2,0:T(8,128)S(1)} custom-call(f32[4,128,128]{2,1,0:T(8,128)} %copy-done.22), custom_call_target="InvertDiagBlocksLowerTriangular" | custom-call | tf_op jit(solution)/shard_map/triangular_solve/custom-call.3 | solution.py:18
  1316.1 27.9 %all-reduce.14.cloned.1.call-done = f32[512,512]{0,1:T(8,128)} async-done(((f32[512,512]{0,1:T(8,128)}), f32[512,512]{0,1:T(8,128)}) %all-reduce.14.cloned.1.call-update) | async-done | bytes 1048592 | tf_op jit(solution)/shard_map/psum | solution.py:9
  1350.5 11.5 while.38
  1362.0 39.7 %custom-call.87 = f32[4,128,128]{1,2,0:T(8,128)S(1)} custom-call(f32[4,128,128]{2,1,0:T(8,128)S(1)} %get-tuple-element.270), custom_call_target="InvertDiagBlocksLowerTriangular" | custom-call | tf_op jit(solution)/shard_map/triangular_solve/custom-call.3 | solution.py:18
  1422.9 39.5 %custom-call.88 = f32[4,128,128]{1,2,0:T(8,128)S(1)} custom-call(f32[4,128,128]{2,1,0:T(8,128)S(1)} %get-tuple-element.271), custom_call_target="InvertDiagBlocksLowerTriangular" | custom-call | tf_op jit(solution)/shard_map/triangular_solve/custom-call.3 | solution.py:18
  1489.5 12.5 while.40
  1502.0 39.3 %custom-call.89 = f32[4,128,128]{1,2,0:T(8,128)S(1)} custom-call(f32[4,128,128]{2,1,0:T(8,128)S(1)} %get-tuple-element.272), custom_call_target="InvertDiagBlocksLowerTriangular" | custom-call | tf_op jit(solution)/shard_map/triangular_solve/custom-call.3 | solution.py:18
  1555.8 13.8 fusion.7
  1569.6 11.9 while.41
  1582.2 40.3 %custom-call.90 = f32[4,128,128]{1,2,0:T(8,128)S(1)} custom-call(f32[4,128,128]{2,1,0:T(8,128)} %copy-done.21), custom_call_target="InvertDiagBlocksLowerTriangular" | custom-call | tf_op jit(solution)/shard_map/triangular_solve/custom-call.3 | solution.py:18
  1650.9 21.0 %fusion.79 = f32[128,2048]{1,0:T(8,128)S(1)} fusion(f32[2048,2048]{1,0:T(8,128)} %constant_dynamic-update-slice_fusion.18, f32[512,2048]{1,0:T(8,128)} %all-gather.3.cloned.1.call-done, s32[]{:T(128)S(6)} %select_n.137), kind=kOutput, calls=%fused_computation.171 | convolution fusion | flops 6442450944 | bytes 18874372 | tf_op jit(solution)/shard_map/dot_general | solution.py:106
  1679.4 10.6 all-to-all-done
  (463 shorter events, 406.7 us)
Async XLA Ops:
  7.2 141.8 %all-gather.3.cloned.1.call-start = ((), (), s32[]{:S(2)}) async-start(), calls=%async_computation.2 | async-start | bytes 5242880 | tf_op jit(solution)/shard_map/all_gather | solution.py:54
  84.0 234.9 %reduce-scatter.4.cloned.1.call-start = ((), (), s32[]{:S(2)}) async-start(), calls=%async_computation.8 | async-start | bytes 4325376 | tf_op jit(solution)/shard_map/reduce_scatter | solution.py:56
  159.1 159.8 %copy-start.23 = (f32[64,512]{1,0:T(8,128)S(1)}, f32[64,512]{1,0:T(8,128)}, u32[]{:S(2)}) copy-start(f32[64,512]{1,0:T(8,128)} %param.42) | copy-start | bytes 393220
  159.1 270.7 %all-gather.5.cloned.1.call-start = ((), (), s32[]{:S(2)}) async-start(), calls=%async_computation.3 | async-start | bytes 4325376 | tf_op jit(solution)/shard_map/all_gather | solution.py:69
  320.5 360.9 %all-reduce.8.cloned.1.call-start = ((), (), s32[]{:S(2)}) async-start(), calls=%async_computation.4 | async-start | bytes 8388608 | tf_op jit(solution)/shard_map/psum | solution.py:9
  438.5 1.0 copy-start.18
  575.8 4.8 copy-start.1
  589.2 331.4 %all-reduce.10.cloned.1.call-start = ((), (), s32[]{:S(2)}) async-start(), calls=%async_computation.5 | async-start | bytes 6291456 | tf_op jit(solution)/shard_map/psum | solution.py:9
  691.8 2.0 copy-start.2
  695.7 1.0 copy-start.19
  833.1 4.8 copy-start.3
  845.0 294.8 %all-reduce.12.cloned.1.call-start = ((), (), s32[]{:S(2)}) async-start(), calls=%async_computation.6 | async-start | bytes 4194304 | tf_op jit(solution)/shard_map/psum | solution.py:9
  929.5 1.7 copy-start.4
  933.1 1.0 copy-start.20
  1071.5 4.8 copy-start.5
  1081.2 262.8 %all-reduce.14.cloned.1.call-start = ((), (), s32[]{:S(2)}) async-start(), calls=%async_computation.7 | async-start | bytes 2097152 | tf_op jit(solution)/shard_map/psum | solution.py:9
  1139.8 7.1 copy-start.8
  1145.5 1.3 copy-start.10
  1236.9 61.1 %copy-start.9 = (f32[1024,512]{0,1:T(8,128)S(1)}, f32[1024,512]{0,1:T(8,128)}, u32[]{:S(2)}) copy-start(f32[1024,512]{0,1:T(8,128)} %slice.852) | copy-start | bytes 6291460
  1249.3 0.7 copy-start.22
  1290.3 7.7 copy-start.11
  1304.1 7.9 copy-start.6
  1312.0 2.6 copy-start.7
  1422.9 41.0 %copy-start.17 = (f32[512,512]{0,1:T(8,128)}, f32[512,512]{0,1:T(8,128)S(1)}, u32[]{:S(2)}) copy-start(f32[512,512]{0,1:T(8,128)S(1)} %get-tuple-element.878) | copy-start | bytes 3145732
  1472.1 3.4 copy-start.14
  1477.4 5.7 copy-start
  1541.8 11.1 copy-start.16
  1581.5 0.7 copy-start.21
  1622.5 7.5 copy-start.15
  1626.7 7.3 copy-start.12
  1637.0 10.0 copy-start.13
  1673.0 17.0 %all-to-all-start = ((f32[128,4,512]{2,0,1:T(8,128)}), f32[128,4,512]{2,0,1:T(8,128)S(1)}, u32[]{:S(2)}, u32[]{:S(2)}) async-start(f32[128,4,512]{2,0,1:T(8,128)} %bitcast.273), calls=%async_computation | async-start | bytes 2097152 | tf_op jit(solution)/shard_map/all_to_all | solution.py:113
Sparse Core Ops, SparseCore 0:
  84.1 64.8 all-gather.2
  159.2 159.6 reduce-scatter.3
  322.5 107.1 all-gather.4
  589.3 91.9 all-reduce.7
  845.1 75.4 all-reduce.9
  1081.3 58.4 all-reduce.11
  1301.2 42.7 all-reduce.13
where the time goes:
time: 1710 us; the launch traced here: 1700 us
  other arithmetic  664 us (39%)
  waiting for transfers between devices  595 us (35%)
  matrix products  205 us (12%)
  local copies, waits for them, and re-layouts  130 us (8%)
  blocking collectives  73.1 us (4%)
  between operations  26.2 us (2%)
    another operation x16, other arithmetic, invert_diag(): lax.linalg.triangular_solve(diag_factor, identity, left_side=True, lower=...  326 us
    another operation x59, other arithmetic, per_device(): diag_factor = jnp.tril(lax.linalg.cholesky(diag_block))  318 us
    psum x4, waiting for transfers between devices, broadcast(): return lax.psum(jnp.where(mine, shard, jnp.zeros_like(shard)), axis)  250 us
    reduce_scatter x1, waiting for transfers between devices, per_device(): lax.psum_scatter(lax.dot_general(full_rows, centered, contract, precision...  160 us
    all_gather x1, waiting for transfers between devices, per_device(): column = lax.all_gather(cov_old + own_rows, 'rows', axis=0, tiled=True)  109 us
    another operation x169, local copies, waits for them, and re-layouts, invert_diag(): lax.linalg.triangular_solve(diag_factor, identity, left_side=True, lower=...  81.2 us
    psum x1, blocking collectives, per_device(): column_sums = lax.psum(jnp.sum(slab, axis=0), 'rows')  73.1 us
    all_gather x1, waiting for transfers between devices, per_device(): full_rows = lax.all_gather(centered, 'feat', axis=1, tiled=True)  65 us
  transfers between devices with their start and end apart: 8, of which 8 were waited for; matrix products, arithmetic and copies ran while one was open for 1% of the time, Pallas kernels for 0%

commit v1 on v0

v1 whole, which is shorter than its diff:
```python
import functools
import jax
import jax.numpy as jnp
from jax import lax
from jax.experimental import pallas as pl
from jax.experimental.pallas import tpu as pltpu
from jax.sharding import PartitionSpec as P

F = jnp.float32
BF = jnp.bfloat16


def sbc(x, j):
    return jnp.broadcast_to(x[j : j + 1, :], (8, 128))


def lbc(x, c):
    return jnp.broadcast_to(x[:, c : c + 1], (8, 128))


def split(x):
    h=x.astype(BF); return h,(x-h.astype(F)).astype(BF)
def mm(a,b): return jnp.dot(a,b,preferred_element_type=F)
def diagC(W,vr=2):
    W=list(W)
    lane=lax.broadcasted_iota(jnp.int32,(8,128),1); sub=lax.broadcasted_iota(jnp.int32,(8,128),0)
    us=[];ls=[]
    C=[lbc(W[0],j) for j in range(8)]
    for k in range(16):
        R=W[k]
        g=8*k
        ing=(lane>=g)&(lane<g+8)
        X=jnp.where(ing,jnp.where(lane-g==sub,1.0,0.0),R); V=R
        FX=X; FV=V
        pv=jnp.ones((8,128),F)
        nxt=k<15
        if nxt:
            Q=[lbc(W[k+1],g+c) for c in range(16)]
            Q0=Q[:8]
        for j in range(0,8,2):
            a=sbc(C[j],j); b=sbc(C[j],j+1); d=sbc(C[j+1],j+1)
            det=a*d-b*b
            rd=1.0/det
            c0=C[j]; c1=C[j+1]
            s0=sub==j; s1=sub==j+1; sp=s0|s1
            n0=jnp.where(s0,-d,jnp.where(s1,b,c0*d-c1*b)); n1=jnp.where(s0,b,jnp.where(s1,-a,c1*a-c0*b))
            m0=n0*rd; m1=n1*rd
            if nxt:
                q0=Q[j]; q1=Q[j+1]
                h0=(q0*d-q1*b)*rd; h1=(q1*a-q0*b)*rd
            def upd(q):
                r0=sbc(q,j); r1=sbc(q,j+1)
                return jnp.where(sp,0.0,q)-(m0*r0+m1*r1), r0, r1
            for c in range(j+2,8):
                C[c],r0,r1=upd(C[c])
                if nxt: Q[c]=Q[c]-(h0*r0+h1*r1)
            if nxt:
                for c in range(8):
                    Q[8+c]=Q[8+c]-(h0*sbc(q0,c)+h1*sbc(q1,c))
            ba=b/a
            X,r0,r1=upd(X)
            FX=jnp.where(s0,r0,jnp.where(s1,r1-ba*r0,FX))
            V,r0,r1=upd(V)
            FV=jnp.where(s0,r0,jnp.where(s1,r1-ba*r0,FV))
            pv=jnp.where(s0,a,jnp.where(s1,d-ba*b,pv))
        Z=X; rs=lax.rsqrt(pv)
        us.append(jnp.where(lane>=g+sub,FV*rs,0.0)); ls.append(jnp.where(lane<=g+sub,FX*rs,0.0))
        zb=[sbc(Z,j) for j in range(8)]
        if nxt: C=Q[8:]
        for i in range(k+1,min(k+1+vr,16)):
            acc=jnp.where(ing,0.0,W[i])
            for j in range(8):
                acc=acc-(Q0[j] if i==k+1 else lbc(W[i],g+j))*zb[j]
            W[i]=acc
        lo=k+1+vr
        if lo<16:
            Wt=jnp.concatenate(W[lo:],axis=0); wh,wl=split(Wt)
            zz=[jnp.zeros((8*k,128),F)] if k else []
            Zf=jnp.concatenate(zz+[Z,jnp.zeros((120-8*k,128),F)],axis=0)
            zh,zl=split(Zf)
            D=mm(wh,zh)+(mm(wh,zl)+mm(wl,zh))
            for i in range(lo,16):
                W[i]=jnp.where(ing,0.0,W[i])-D[8*(i-lo):8*(i-lo)+8]
    return us,ls

BLK={(1,0):0,(2,0):1,(3,0):2,(2,1):3,(3,1):4,(3,2):5}
def nt(a,b): return lax.dot_general(a,b,(((1,),(1,)),((),())),preferred_element_type=F)
def nt3(ah,al,bh,bl): return nt(ah,bh)+(nt(ah,bl)+nt(al,bh))
def nn3(ah,al,bh,bl): return mm(ah,bh)+(mm(ah,bl)+mm(al,bh))
def gtile(g_ref,I,J,t):
    if I==J: return g_ref[J,pl.ds(16*t,16),0:16,:].reshape(256,512)
    if (I,J)==(3,0): return g_ref[3,pl.ds(16*t,16),16:32,:].reshape(256,512)
    if I==J+1: return g_ref[J,pl.ds(16*t,16),16:32,:].reshape(256,512)
    return g_ref[J+2*t,:,32:40,:].reshape(256,512)
def k3(s_ref,g_ref,c_ref,y_ref,f_ref,S,UR,XH,XL,LF,LH,LL,YH,YL):
    f=s_ref[0]; blk=s_ref[1]; sb=s_ref[2]
    for J in range(4):
        @pl.loop(0,2)
        def _(t):
            acc=gtile(g_ref,J,J,t)
            rows=pl.ds(pl.multiple_of(256*t,256),256)
            for K in range(J):
                q=BLK[(J,K)]
                acc=acc-nt3(LH[q,rows,:],LL[q,rows,:],LH[q],LL[q])
            for u in range(2):
                for c in range(4):
                    S[2*t+u,c]=acc[128*u:128*u+128,128*c:128*c+128]
        lane=lax.broadcasted_iota(jnp.int32,(128,128),1); row=lax.broadcasted_iota(jnp.int32,(128,128),0)
        @pl.loop(0,4)
        def _(b):
            D=S[b,b]
            us,ls=diagC([D[8*k:8*k+8] for k in range(16)])
            li=jnp.concatenate(ls,axis=0)
            LF[J,J,b,b]=jnp.concatenate(us,axis=0).T
            S[b,b]=jnp.where(lane==row,1.0,0.0)
            lh,ll=split(li)
            rr=jnp.concatenate([S[b,c] for c in range(4)],axis=1)
            rh,rl=split(rr)
            ur=nn3(lh,ll,rh,rl)
            for c in range(4):
                UR[b,c]=jnp.where(c<=b,ur[:,128*c:128*c+128],0.0)
            uh,ul=split(ur)
            @pl.loop(b+1,4)
            def _(i):
                ph,plo=split(S[i,b])
                p=nt3(ph,plo,lh,ll)
                LF[J,J,i,b]=p
                LF[J,J,b,i]=jnp.zeros((128,128),F)
                S[i,b]=jnp.zeros((128,128),F)
                ph,plo=split(p)
                d=nn3(ph,plo,uh,ul)
                for c in range(4):
                    S[i,c]=S[i,c]-d[:,128*c:128*c+128]
        for b in range(4):
            x=jnp.concatenate([UR[b,c] for c in range(4)],axis=1)
            h,l=split(x)
            XH[128*b:128*b+128,:]=h; XL[128*b:128*b+128,:]=l
        for I in range(J+1,4):
            @pl.loop(0,2)
            def _(t):
                acc=gtile(g_ref,I,J,t)
                rows=pl.ds(pl.multiple_of(256*t,256),256)
                for K in range(J):
                    q=BLK[(I,K)]; w=BLK[(J,K)]
                    acc=acc-nt3(LH[q,rows,:],LL[q,rows,:],LH[w],LL[w])
                ah,al=split(acc)
                p=nt3(ah,al,XH[...],XL[...])
                for u in range(2):
                    for c in range(4):
                        LF[I,J,2*t+u,c]=p[128*u:128*u+128,128*c:128*c+128]
                h,l=split(p)
                q=BLK[(I,J)]
                LH[q,rows,:]=h; LL[q,rows,:]=l
        @pl.when(f>=J)
        def _():
            @pl.loop(0,2)
            def _(t):
                rows=pl.ds(pl.multiple_of(256*t,256),256)
                acc=c_ref[J,rows,:]
                for K in range(J):
                    w=BLK[(J,K)]
                    acc=acc-nt3(YH[K,rows,:],YL[K,rows,:],LH[w],LL[w])
                ah,al=split(acc)
                p=nt3(ah,al,XH[...],XL[...])
                y_ref[rows,:]=p
                if J<3:
                    h,l=split(p)
                    YH[J,rows,:]=h; YL[J,rows,:]=l
    half=pl.ds(pl.multiple_of(64*(sb%2),64),64)
    for c in range(4):
        f_ref[:,128*c:128*c+128]=jnp.where(blk>=f,LF[blk,f,sb//2,c,half,:],0.0)
def k3call(s,g,c):
    V=pltpu.VMEM
    return pl.pallas_call(k3,out_shape=[jax.ShapeDtypeStruct((512,512),F),jax.ShapeDtypeStruct((64,512),F)],
        in_specs=[pl.BlockSpec(memory_space=pltpu.SMEM),pl.BlockSpec(memory_space=V),pl.BlockSpec(memory_space=V)],
        out_specs=[pl.BlockSpec(memory_space=V)]*2,
        scratch_shapes=[V((4,4,128,128),F),V((4,4,128,128),F),V((512,512),BF),V((512,512),BF),V((4,4,4,4,128,128),F),
            V((6,512,512),BF),V((6,512,512),BF),V((3,512,512),BF),V((3,512,512),BF)],
        compiler_params=pltpu.CompilerParams(vmem_limit_bytes=60*2**20))(s,g,c)


def dot_t(a, b):
    return lax.dot_general(
        a, b, (((0,), (0,)), ((), ())), precision=lax.Precision.HIGHEST, preferred_element_type=F
    )


def per_device(slab, cov_old):
    n_rows = lax.axis_size("rows")
    r = lax.axis_index("rows")
    f = lax.axis_index("feat")
    rows_dev, width = slab.shape
    total = rows_dev * n_rows
    blk = r // 8
    sub = r % 8
    sums = lax.psum(jnp.sum(slab, axis=0), "rows")
    centered = slab - (sums / total)[None, :]
    c = lax.all_gather(centered, "feat", axis=0)
    pick = lambda i: lax.dynamic_index_in_dim(c, i, 0, keepdims=False)
    o_row = jnp.minimum(f + 1, 3)
    o_col = jnp.where(f < 3, f, 0)
    h_row = jnp.where(f < 2, f + 2, f)
    h_col = jnp.where(f < 2, f, f - 2)
    h_low = jnp.where(f < 2, 0, 256)
    left_h = lax.dynamic_slice_in_dim(pick(h_row), h_low, 256, 1)
    base = lax.dynamic_update_slice_in_dim(jnp.zeros((512, 512), F), cov_old, 64 * sub, 0)
    base_t = base.T
    zero = jnp.zeros((), F)
    d = dot_t(centered, centered) / total + jnp.where(blk == f, base, zero)
    o = dot_t(pick(o_row), pick(o_col)) / total
    o += jnp.where(f < 3, jnp.where(blk == f + 1, base, zero), jnp.where(blk == 0, base_t, zero))
    h = dot_t(left_h, pick(h_col)) / total
    h += jnp.where(
        f < 2,
        jnp.where(blk == f + 2, base[:256], zero),
        jnp.where(blk == f - 2, base_t[256:], zero),
    )
    parts = jnp.concatenate(
        [d.reshape(32, 16, 512), o.reshape(32, 16, 512), h.reshape(32, 8, 512)], axis=1
    )
    mine = lax.psum_scatter(parts, "rows", scatter_dimension=0, tiled=False)
    g = lax.all_gather(mine, "rows", axis=0)
    g = lax.all_gather(g, "feat", axis=0)
    s = jnp.stack([f, blk, sub]).astype(jnp.int32)
    y, fac = k3call(s, g, c)
    return (y, fac)


def solution(mesh):
    placed = (P("rows", "feat"), P("rows", "feat"))
    return jax.shard_map(
        per_device, mesh=mesh, in_specs=placed, out_specs=placed, check_vma=False
    )
```

time: 1710 us -> 619 us (0.36)
  other arithmetic: 664 us -> 6.13 us
  matrix products: 205 us -> 9.17 us
  waiting for transfers between devices: 595 us -> 420 us
  local copies, waits for them, and re-layouts: 130 us -> 1.04 us
  Pallas kernels: 0 us -> 95 us
    another operation x77 -> x1, other arithmetic: 648 us -> 0.61 us  [per_device(): s = jnp.stack([f, blk, sub]).astype(jnp.int32)]
    psum x4 -> x0, waiting for transfers between devices: 250 us -> none  [broadcast(): return lax.psum(jnp.where(mine, shard, jnp.zeros_like(shard)), axis)]
    dot_general x21 -> x3, matrix products: 134 us -> 9.17 us  [dot_t(): lax.dot_general(a, b, (((0,), (0,)), ((), ())), precision=lax.Precision.H...]
    pallas_call x0 -> x1, Pallas kernels: none -> 95 us  [k3call(): pl.pallas_call(k3, out_shape=[jax.ShapeDtypeStruct((512, 512), F), jax.Sh...]
    all_gather x2 -> x3, waiting for transfers between devices: 174 us -> 265 us  [the longest x1 102 us: per_device(): g = lax.all_gather(mine, 'rows', axis=0)]
    another operation x221 -> x0, local copies, waits for them, and re-layouts: 84.1 us -> none  [the longest x169 81.2 us: invert_diag(): lax.linalg.triangular_solve(diag_factor, identity, left_side=True, lower=...]
    another operation x80 -> x0, matrix products: 70.4 us -> none  [the longest x56 50 us: invert_diag(): lax.linalg.triangular_solve(diag_factor, identity, left_side=True, lower=...]
  transfers between devices with their start and end apart: 8 -> 4, of which waited for: 8 -> 4; matrix products, arithmetic and copies ran while one was open for 1% -> 1% of each run, Pallas kernels for 0% -> 0%
where the time goes in v1:
time: 619 us; the launch traced here: 618 us
  waiting for transfers between devices  420 us (68%)
  Pallas kernels  95 us (15%)
  blocking collectives  73.1 us (12%)
  between operations  13.9 us (2%)
  matrix products  9.17 us (1%)
    reduce_scatter x1, waiting for transfers between devices, per_device(): mine = lax.psum_scatter(parts, 'rows', scatter_dimension=0, tiled=False)  155 us
    all_gather x1, waiting for transfers between devices, per_device(): g = lax.all_gather(mine, 'rows', axis=0)  102 us
    all_gather x1, waiting for transfers between devices, per_device(): g = lax.all_gather(g, 'feat', axis=0)  101 us
    pallas_call x1, Pallas kernels, k3call(): pl.pallas_call(k3, out_shape=[jax.ShapeDtypeStruct((512, 512), F), jax.Sh...  95 us
    psum x1, blocking collectives, per_device(): sums = lax.psum(jnp.sum(slab, axis=0), 'rows')  73.1 us
    all_gather x1, waiting for transfers between devices, per_device(): c = lax.all_gather(centered, 'feat', axis=0)  61 us
  transfers between devices with their start and end apart: 4, of which 4 were waited for; matrix products, arithmetic and copies ran while one was open for 1% of the time, Pallas kernels for 0%

profile of v1, /device:TPU:7, one launch (start us, length us, event | category | flops | bytes accessed | tf_op | source)
XLA Modules:
  0.0 618.3 jit_solution(263179656340316234)
XLA Ops:
  7.2 0.0 copy-start.2
  7.2 0.0 all-gather.8.cloned.1.call-start
  7.2 1.4 reduce_sum.9
  8.6 73.1 %psum.7 = f32[512]{0:T(512)S(1)} all-reduce(f32[512]{0:T(512)S(1)} %reduce_sum.9), channel_id=1, replica_groups=mesh['rows'=32,'feat'=4] {'rows'}, use_global_device_ids=true, to_apply=%region_1.2 | all-reduce | flops 512 | bytes 4096 | tf_op jit(solution)/shard_map/psum | solution.py:196
  81.7 2.3 broadcast_subtract_fusion
  84.0 0.0 copy-start
  84.0 0.0 all-gather.8.cloned.1.call-update
  84.0 0.0 reduce-scatter.2.cloned.1.call-start
  84.1 0.1 broadcast_in_dim.13
  84.3 0.0 copy-done.2
  84.3 0.3 copy.5
  84.6 0.6 copy-done
  85.2 2.8 fusion.1
  88.0 61.0 %all-gather.8.cloned.1.call-done = f32[2048,512]{1,0:T(8,128)} async-done(((f32[512,512]{1,0:T(8,128)}), f32[2048,512]{1,0:T(8,128)}) %all-gather.8.cloned.1.call-update) | async-done | bytes 4194320 | tf_op jit(solution)/shard_map/all_gather | solution.py:198
  149.0 0.0 copy-start.1
  149.0 3.5 fusion
  152.6 2.8 fusion.3
  155.4 0.0 copy-done.1
  155.4 1.8 pad_maximum_fusion
  157.2 0.0 reduce-scatter.2.cloned.1.call-update
  157.2 0.0 all-gather.6.cloned.1.call-start
  157.3 155.2 %reduce-scatter.2.cloned.1.call-done = f32[1,40,512]{2,1,0:T(8,128)} async-done(((f32[32,40,512]{2,1,0:T(8,128)}), f32[1,40,512]{2,1,0:T(8,128)}) %reduce-scatter.2.cloned.1.call-update) | async-done | bytes 81936 | tf_op jit(solution)/shard_map/reduce_scatter | solution.py:221
  312.4 0.0 all-gather.6.cloned.1.call-update
  312.4 0.0 all-gather.10.cloned.1.call-start
  312.5 102.3 %all-gather.6.cloned.1.call-done = f32[32,40,512]{2,1,0:T(8,128)} async-done(((f32[1,40,512]{2,1,0:T(8,128)}), f32[32,40,512]{2,1,0:T(8,128)}) %all-gather.6.cloned.1.call-update) | async-done | bytes 2621456 | tf_op jit(solution)/shard_map/all_gather | solution.py:222
  414.8 0.0 all-gather.10.cloned.1.call-update
  414.9 0.6 pad_add_fusion.s_ref
  415.5 101.4 %all-gather.10.cloned.1.call-done = f32[128,40,512]{2,1,0:T(8,128)} async-done(((f32[32,40,512]{2,1,0:T(8,128)}), f32[128,40,512]{2,1,0:T(8,128)}) %all-gather.10.cloned.1.call-update) | async-done | bytes 10485776 | tf_op jit(solution)/shard_map/all_gather | solution.py:223
  516.8 95.0 %shard_map.41 = (f32[512,512]{1,0:T(8,128)}, f32[64,512]{1,0:T(8,128)}) custom-call(s32[3]{0:T(128)} %pad_add_fusion.s_ref, f32[4,32,40,512]{3,2,1,0:T(8,128)} %bitcast.28, f32[4,512,512]{2,1,0:T(8,128)} %bitcast.27), custom_call_target="tpu_custom_call" | custom-call | tf_op jit(solution)/shard_map/pallas_call | solution.py:174
  (2 shorter events, 0.0 us)
Async XLA Ops:
  7.2 77.1 %copy-start.2 = (f32[64,512]{1,0:T(8,128)S(1)}, f32[64,512]{1,0:T(8,128)}, u32[]{:S(2)}) copy-start(f32[64,512]{1,0:T(8,128)} %param.3) | copy-start | bytes 393220
  7.2 141.8 %all-gather.8.cloned.1.call-start = ((), (), s32[]{:S(2)}) async-start(), calls=%async_computation.3 | async-start | bytes 5242880 | tf_op jit(solution)/shard_map/all_gather | solution.py:198
  84.0 1.2 copy-start
  84.0 228.4 %reduce-scatter.2.cloned.1.call-start = ((), (), s32[]{:S(2)}) async-start(), calls=%async_computation.1 | async-start | bytes 2703360 | tf_op jit(solution)/shard_map/reduce_scatter | solution.py:221
  149.0 6.3 %copy-start.1 = (f32[512,512]{1,0:T(8,128)S(1)}, f32[512,512]{1,0:T(8,128)}, u32[]{:S(2)}) copy-start(f32[512,512]{1,0:T(8,128)} %fusion.1) | copy-start | bytes 3145732
  157.2 257.6 %all-gather.6.cloned.1.call-start = ((), (), s32[]{:S(2)}) async-start(), calls=%async_computation.2 | async-start | bytes 2703360 | tf_op jit(solution)/shard_map/all_gather | solution.py:222
  312.4 204.4 %all-gather.10.cloned.1.call-start = ((), (), s32[]{:S(2)}) async-start(), calls=%async_computation.4 | async-start | bytes 13107200 | tf_op jit(solution)/shard_map/all_gather | solution.py:223
Sparse Core Ops, SparseCore 0:
  84.1 64.8 all-gather.7
  157.3 155.0 reduce-scatter.1
  315.5 99.2 all-gather.5
  416.3 100.4 all-gather.9

commit v2 on v1

--- a/solution.py
+++ b/solution.py
@@ -179,6 +179,196 @@
         compiler_params=pltpu.CompilerParams(vmem_limit_bytes=60*2**20))(s,g,c)
 
 
+MESH = pl.DeviceIdType.MESH
+
+
+def remote(src, dst, send, recv, rows, feat):
+    return pltpu.make_async_remote_copy(
+        src_ref=src, dst_ref=dst, send_sem=send, recv_sem=recv,
+        device_id=(rows, feat), device_id_type=MESH,
+    )
+
+
+def greet(peers):
+    barrier = pltpu.get_barrier_semaphore()
+    for rows, feat in peers:
+        pl.semaphore_signal(barrier, inc=1, device_id=(rows, feat), device_id_type=MESH)
+    pl.semaphore_wait(barrier, len(peers))
+
+
+def gather_kernel(slab, c, m, sums, own, s_send, s_recv, m_send, m_recv, x_send, x_recv, b_send, b_recv, f_send, f_recv):
+    r = lax.axis_index("rows")
+    f = lax.axis_index("feat")
+    core = f % 2
+    side = f // 2
+    sib = 2 * side + 1 - core
+    opp = 2 * (1 - side) + core
+    feats = [(f + d) % 4 for d in range(1, 4)]
+    greet([((r + d) % 32, f) for d in range(1, 32)] + [(r, g) for g in feats])
+    across = []
+    for q in range(4):
+        part = pl.ds(128 * q, 128)
+        cp = remote(slab.at[part], c.at[f, part], x_send.at[q], x_recv.at[q], r, opp)
+        cp.start()
+        across.append(cp)
+    beside = remote(slab, c.at[f], b_send, b_recv, r, sib)
+    beside.start()
+    keep = pltpu.make_async_copy(slab, c.at[f], own)
+    keep.start()
+    sums[r] = jnp.sum(slab[...], axis=0, keepdims=True)
+    sent = []
+    for d in range(1, 32):
+        cp = remote(sums.at[r], sums.at[r], s_send.at[d], s_recv.at[d], (r + d) % 32, f)
+        cp.start()
+        sent.append(cp)
+    for cp in sent:
+        cp.wait_recv()
+    m[f] = jnp.sum(sums[...], axis=0) * (1.0 / 16384.0)
+    shared = []
+    for d in range(1, 4):
+        cp = remote(m.at[f], m.at[f], m_send.at[d], m_recv.at[d], r, (f + d) % 4)
+        cp.start()
+        shared.append(cp)
+    passed = []
+    for q in range(4):
+        part = pl.ds(128 * q, 128)
+        across[q].wait_recv()
+        cp = remote(c.at[opp, part], c.at[opp, part], f_send.at[q], f_recv.at[q], r, sib)
+        cp.start()
+        passed.append(cp)
+    for cp in sent + across:
+        cp.wait_send()
+    for cp in shared + passed + [beside, keep]:
+        cp.wait()
+
+
+def gather(slab):
+    D = pltpu.SemaphoreType.DMA
+    V = pltpu.VMEM
+    return pl.pallas_call(
+        gather_kernel,
+        out_shape=[jax.ShapeDtypeStruct((4, 512, 512), F), jax.ShapeDtypeStruct((4, 1, 512), F)],
+        in_specs=[pl.BlockSpec(memory_space=V)],
+        out_specs=[pl.BlockSpec(memory_space=V)] * 2,
+        scratch_shapes=[V((32, 1, 512), F), D(()), D((32,)), D((32,)), D((4,)), D((4,)), D((4,)), D((4,)), D(()), D(()), D((4,)), D((4,))],
+        compiler_params=pltpu.CompilerParams(collective_id=1, has_side_effects=True, vmem_limit_bytes=24 * 2**20),
+    )(slab)
+
+
+PIECE = ((0, 16), (16, 16), (32, 8))
+ORDER = (("y", "z", "x"), ("z", "x", "y"), ("x", "y", "z"))
+
+
+def reduce_kernel(parts, g, inbox, mine, p_send, p_recv, own, a_send, a_recv, c_send, c_recv):
+    r = lax.axis_index("rows")
+    f = lax.axis_index("feat")
+    core = f % 2
+    at = {"z": r // 8, "x": 2 * ((r // 4) % 2) + f // 2, "y": r % 4}
+
+    def place(pos, cr):
+        return (pos["z"] * 2 + pos["x"] // 2) * 4 + pos["y"], (pos["x"] % 2) * 2 + cr
+
+    def moved(dim, by):
+        pos = dict(at)
+        pos[dim] = (at[dim] + by + 4) % 4
+        return pos
+
+    sib = place(at, 1 - core)
+    greet([((r + d) % 32, f) for d in range(1, 32)] + [place(moved("x", 1), core), place(moved("x", -1), core), sib])
+    sent = []
+    for d in range(1, 32):
+        to = (r + d) % 32
+        cp = remote(parts.at[to], inbox.at[d], p_send.at[d], p_recv.at[d], to, f)
+        cp.start()
+        sent.append(cp)
+    for cp in sent:
+        cp.wait_recv()
+    total = parts[r]
+    for d in range(1, 32):
+        total = total + inbox[d]
+    mine[...] = total
+
+    def view(ref, piece, pos, full, lanes=(0, 512)):
+        a, n = PIECE[piece]
+        every = pl.ds(0, 4)
+        two = pl.ds(0, 2)
+        xl = two if "x" in full else pos["x"] % 2
+        xh = two if "x" in full else pos["x"] // 2
+        zz = every if "z" in full else pos["z"]
+        yy = every if "y" in full else pos["y"]
+        return ref.at[xl, core, zz, xh, yy, pl.ds(a, n), pl.ds(lanes[0], lanes[1])]
+
+    pending = []
+    count = [0]
+
+    def pass_on(piece, pos, full):
+        k = count[0]
+        count[0] += 1
+        v = view(g, piece, pos, full)
+        cp = remote(v, v, c_send.at[k], c_recv.at[k], *sib)
+        cp.start()
+        pending.append(cp)
+
+    for p in range(3):
+        a, n = PIECE[p]
+        cp = pltpu.make_async_copy(mine.at[pl.ds(a, n)], view(g, p, at, ()), own.at[p])
+        cp.start()
+        cp.wait()
+    for s in range(3):
+        first = []
+        for p in range(3):
+            dim = ORDER[p][s]
+            full = ORDER[p][:s]
+            v = view(g, p, at, full)
+            pair = []
+            for way, by in enumerate((1, -1)):
+                k = (p * 3 + s) * 4 + way
+                cp = remote(v, v, a_send.at[k], a_recv.at[k], *place(moved(dim, by), core))
+                cp.start()
+                pair.append(cp)
+            first.append(pair)
+            if s == 0:
+                pass_on(p, at, ())
+        second = []
+        for p in range(3):
+            dim = ORDER[p][s]
+            full = ORDER[p][:s]
+            pair = []
+            for way, by in enumerate((1, -1)):
+                first[p][way].wait_recv()
+                k = (p * 3 + s) * 4 + 2 + way
+                v = view(g, p, moved(dim, -by), full, (256 * way, 256))
+                cp = remote(v, v, a_send.at[k], a_recv.at[k], *place(moved(dim, by), core))
+                cp.start()
+                pair.append(cp)
+            second.append(pair)
+            for by in (-1, 1):
+                pass_on(p, moved(dim, by), full)
+        for p in range(3):
+            for cp in second[p]:
+                cp.wait_recv()
+            pass_on(p, moved(ORDER[p][s], 2), ORDER[p][:s])
+            for cp in first[p] + second[p]:
+                cp.wait_send()
+    for cp in pending:
+        cp.wait()
+    for cp in sent:
+        cp.wait_send()
+
+
+def reduce_gather(parts):
+    D = pltpu.SemaphoreType.DMA
+    V = pltpu.VMEM
+    return pl.pallas_call(
+        reduce_kernel,
+        out_shape=jax.ShapeDtypeStruct((2, 2, 4, 2, 4, 40, 512), F),
+        in_specs=[pl.BlockSpec(memory_space=V)],
+        out_specs=pl.BlockSpec(memory_space=pl.ANY),
+        scratch_shapes=[V((32, 40, 512), F), V((40, 512), F), D((32,)), D((32,)), D((3,)), D((36,)), D((36,)), D((30,)), D((30,))],
+        compiler_params=pltpu.CompilerParams(collective_id=2, has_side_effects=True, vmem_limit_bytes=24 * 2**20),
+    )(parts)
+
+
 def dot_t(a, b):
     return lax.dot_general(
         a, b, (((0,), (0,)), ((), ())), precision=lax.Precision.HIGHEST, preferred_element_type=F
@@ -193,9 +383,8 @@
     total = rows_dev * n_rows
     blk = r // 8
     sub = r % 8
-    sums = lax.psum(jnp.sum(slab, axis=0), "rows")
-    centered = slab - (sums / total)[None, :]
-    c = lax.all_gather(centered, "feat", axis=0)
+    raw, means = gather(slab)
+    c = raw - means
     pick = lambda i: lax.dynamic_index_in_dim(c, i, 0, keepdims=False)
     o_row = jnp.minimum(f + 1, 3)
     o_col = jnp.where(f < 3, f, 0)
@@ -206,6 +395,7 @@
     base = lax.dynamic_update_slice_in_dim(jnp.zeros((512, 512), F), cov_old, 64 * sub, 0)
     base_t = base.T
     zero = jnp.zeros((), F)
+    centered = pick(f)
     d = dot_t(centered, centered) / total + jnp.where(blk == f, base, zero)
     o = dot_t(pick(o_row), pick(o_col)) / total
     o += jnp.where(f < 3, jnp.where(blk == f + 1, base, zero), jnp.where(blk == 0, base_t, zero))
@@ -218,9 +408,7 @@
     parts = jnp.concatenate(
         [d.reshape(32, 16, 512), o.reshape(32, 16, 512), h.reshape(32, 8, 512)], axis=1
     )
-    mine = lax.psum_scatter(parts, "rows", scatter_dimension=0, tiled=False)
-    g = lax.all_gather(mine, "rows", axis=0)
-    g = lax.all_gather(g, "feat", axis=0)
+    g = reduce_gather(parts).reshape(4, 32, 40, 512)
     s = jnp.stack([f, blk, sub]).astype(jnp.int32)
     y, fac = k3call(s, g, c)
     return (y, fac)

time: 619 us -> 234 us (0.38)
  waiting for transfers between devices: 420 us -> 0 us
  Pallas kernels: 95 us -> 221 us
  blocking collectives: 73.1 us -> 0 us
  between operations: 13.9 us -> 0.82 us
    all_gather x3 -> x0, waiting for transfers between devices: 265 us -> none  [the longest x1 102 us: per_device(): g = lax.all_gather(mine, 'rows', axis=0)]
    reduce_scatter x1 -> x0, waiting for transfers between devices: 155 us -> none  [per_device(): mine = lax.psum_scatter(parts, 'rows', scatter_dimension=0, tiled=False)]
    pallas_call x0 -> x2, Pallas kernels: none -> 126 us  [the longest x1 87.5 us: reduce_gather(): pl.pallas_call(reduce_kernel, out_shape=jax.ShapeDtypeStruct((2, 2, 4, 2,...]
    psum x1 -> x0, blocking collectives: 73.1 us -> none  [per_device(): sums = lax.psum(jnp.sum(slab, axis=0), 'rows')]
  transfers between devices with their start and end apart: 4 -> 0, of which waited for: 4 -> 0; matrix products, arithmetic and copies ran while one was open for 1% -> 0% of each run, Pallas kernels for 0% -> 0%
where the time goes in v2:
time: 234 us
  Pallas kernels  221 us (94%)
  local copies, waits for them, and re-layouts  5.34 us (2%)
  matrix products  5.32 us (2%)
    pallas_call x1, Pallas kernels, k3call(): pl.pallas_call(k3, out_shape=[jax.ShapeDtypeStruct((512, 512), F), jax.Sh...  95 us
    pallas_call x1, Pallas kernels, reduce_gather(): pl.pallas_call(reduce_kernel, out_shape=jax.ShapeDtypeStruct((2, 2, 4, 2,...  87.5 us
    pallas_call x1, Pallas kernels, gather(): pl.pallas_call(gather_kernel, out_shape=[jax.ShapeDtypeStruct((4, 512, 51...  38.7 us
    dot_general x3, matrix products, dot_t(): lax.dot_general(a, b, (((0,), (0,)), ((), ())), precision=lax.Precision.H...  5.32 us

profile of v2, /device:TPU:7, one launch (start us, length us, event | category | flops | bytes accessed | tf_op | source)
XLA Modules:
  0.0 234.1 jit_solution(154800598198122002)
XLA Ops:
  0.6 0.0 copy-start.1
  0.7 0.7 pad_add_fusion.s_ref
  1.4 0.1 broadcast_in_dim.12
  1.5 0.9 constant_dynamic-update-slice_fusion
  2.4 0.3 copy.4
  2.8 0.0 copy-done.1
  2.8 38.7 %shard_map.41 = (f32[4,512,512]{2,1,0:T(8,128)S(1)}, f32[4,1,512]{2,1,0:T(1,128)S(1)}) custom-call(f32[512,512]{1,0:T(8,128)S(1)} %copy-done.1), custom_call_target="tpu_custom_call" | custom-call | tf_op jit(solution)/shard_map/pallas_call | solution.py:248
  41.5 0.5 broadcast_subtract_fusion.c_ref
  42.1 0.0 copy-start.2
  42.1 1.4 fusion.3
  43.5 2.0 fusion
  45.5 0.0 copy-done.2
  45.5 1.9 fusion.1
  47.5 0.2 pad_maximum_fusion.parts
  47.7 87.5 %shard_map.42 = f32[2,2,4,2,4,40,512]{6,5,4,3,2,1,0:T(8,128)S(1)} custom-call(f32[32,40,512]{2,1,0:T(8,128)S(1)} %pad_maximum_fusion.parts), custom_call_target="tpu_custom_call" | custom-call | tf_op jit(solution)/shard_map/pallas_call | solution.py:362
  135.2 0.0 copy-start
  135.2 4.0 %copy-done = f32[2,2,4,2,4,40,512]{6,5,4,3,2,1,0:T(8,128)} copy-done((f32[2,2,4,2,4,40,512]{6,5,4,3,2,1,0:T(8,128)}, f32[2,2,4,2,4,40,512]{6,5,4,3,2,1,0:T(8,128)S(1)}, u32[]{:S(2)}) %copy-start) | copy-done | bytes 10485784
  139.2 95.0 %shard_map.43 = (f32[512,512]{1,0:T(8,128)}, f32[64,512]{1,0:T(8,128)}) custom-call(s32[3]{0:T(128)} %pad_add_fusion.s_ref, f32[4,32,40,512]{3,2,1,0:T(8,128)} %bitcast.28, f32[4,512,512]{2,1,0:T(8,128)} %copy-done.2), custom_call_target="tpu_custom_call" | custom-call | tf_op jit(solution)/shard_map/pallas_call | solution.py:174
  (1 shorter events, 0.0 us)
Async XLA Ops:
  0.6 2.1 copy-start.1
  42.1 3.4 %copy-start.2 = (f32[4,512,512]{2,1,0:T(8,128)}, f32[4,512,512]{2,1,0:T(8,128)S(1)}, u32[]{:S(2)}) copy-start(f32[4,512,512]{2,1,0:T(8,128)S(1)} %broadcast_subtract_fusion.c_ref) | copy-start | bytes 12582916
  135.2 4.0 %copy-start = (f32[2,2,4,2,4,40,512]{6,5,4,3,2,1,0:T(8,128)}, f32[2,2,4,2,4,40,512]{6,5,4,3,2,1,0:T(8,128)S(1)}, u32[]{:S(2)}) copy-start(f32[2,2,4,2,4,40,512]{6,5,4,3,2,1,0:T(8,128)S(1)} %shard_map.42) | copy-start | bytes 31457284
